TPU v7x, 1024 devices: a whole 4x8x16 slice. The times are simulated.
1024 devices in a mesh: seq: 16 (over y, core), head: 4 (over x), dp: 16 (over z).
Axes of the slice: x: 4, y: 8, z: 16, core: 2. Of those that a mesh axis runs over, the one named last changes fastest.
Arguments:
- queries: bfloat16 [16, 3584, 4096], P('dp', 'seq', 'head'), may hold values from -6 to 6
- keys_in: bfloat16 [16, 3584, 4096], P('dp', 'seq', 'head'), may hold values from -6 to 6
- values_in: bfloat16 [16, 3584, 4096], P('dp', 'seq', 'head'), may hold values from -6 to 6
- grad_output: bfloat16 [16, 3584, 4096], P('dp', 'seq', 'head'), may hold values from -6 to 6
- log_decay: float32 [16, 3584, 32], P('dp', 'seq', 'head'), may hold values from -1 to 0, as said below
- doc_lengths: int32 [16, 4], P('dp'), may hold values from 1 to 1792, 3584 in all within a row
- norm_gain: float32 [4096], P('head'), may hold values from 0.1 to 1.9
Outputs:
- query_grad: bfloat16 [16, 3584, 4096], P('dp', 'seq', 'head')
- key_grad: bfloat16 [16, 3584, 4096], P('dp', 'seq', 'head')
- value_grad: bfloat16 [16, 3584, 4096], P('dp', 'seq', 'head')
- gain_grad: float32 [4096], P('head')
Inputs may be any that keep to these rules, and one draw needn't show every extreme that they name: `doc_lengths`: each row holds 4 lengths that sum to 3584; the largest is exactly 1792. `log_decay`: every entry is negative.
All inputs are finite; a program needn't handle non-finite values.
Results may differ from a plain program's by a relative error of at most 0.0062.
Values sent between devices are 32-bit elements; how exact they have to be, the bound alone decides.
A program may use at most 64 MiB of HBM per device.

v0:
```python
import math

import jax
import jax.numpy as jnp
from jax import lax
from jax.sharding import PartitionSpec as P

BLK = 224


EPSILON = 1e-06


def entering(value, axis, join, neutral, backward):
    count, mine = (lax.axis_size(axis), lax.axis_index(axis))
    pieces = jax.tree.map(lambda part: lax.all_gather(part, axis), value)
    if backward:
        pieces = jax.tree.map(lambda part: part[::-1], pieces)
        mine = count - 1 - mine
    subtotal = jax.tree.map(
        lambda part, zero: jnp.full_like(part, 0) + jnp.asarray(zero, part.dtype), value, neutral
    )

    def turn(position, subtotal):
        longer = join(subtotal, jax.tree.map(lambda part: part[position], pieces))
        return jax.tree.map(lambda new, old: jnp.where(position < mine, new, old), longer, subtotal)

    return lax.fori_loop(0, count - 1, turn, subtotal)


def widen(array):
    return array.astype(jnp.float32)


def block_terms(log_decay, resets):
    nblk, blk, heads = log_decay.shape
    zcount = jnp.cumsum(resets.astype(jnp.int32), axis=1, dtype=jnp.int32)
    cumlog = jnp.cumsum(log_decay, axis=1)
    keeping = (zcount == 0).astype(jnp.float32)
    entry = jnp.exp(cumlog) * keeping[:, :, None]
    tail = cumlog[:, -1:, :]
    ending = (zcount == zcount[:, -1:]).astype(jnp.float32)
    leaving = jnp.exp(tail - cumlog) * ending[:, :, None]
    carry_factor = jnp.exp(tail[:, 0, :]) * keeping[:, -1:]
    row_index = lax.broadcasted_iota(jnp.int32, (blk, blk), 0)
    col_index = lax.broadcasted_iota(jnp.int32, (blk, blk), 1)
    allowed = (zcount[:, :, None] == zcount[:, None, :]) & (col_index <= row_index)[None]
    allowed = allowed[:, None]
    by_head = jnp.transpose(cumlog, (0, 2, 1))
    spread = by_head[:, :, :, None] - by_head[:, :, None, :]
    decay_mask = jnp.where(allowed, jnp.exp(jnp.where(allowed, spread, 0.0)), 0.0)
    return (entry, leaving, carry_factor, decay_mask)


def forward_blocks(query, keys, values, entry, leaving, decay_mask):
    scores = jnp.einsum("bthd,bshd->bhts", widen(query), widen(keys))
    weights = (scores * decay_mask).astype(jnp.bfloat16)
    query_entry = (query * entry[..., None]).astype(jnp.bfloat16)
    key_leave = (keys * leaving[..., None]).astype(jnp.bfloat16)
    block_state = jnp.einsum("bshi,bshj->bhij", widen(key_leave), widen(values))
    return (weights, query_entry, block_state)


def chain_states(carry_factor, updates, initial, backward):

    def advance(state, pair):
        factor, update = pair
        return (factor[:, None, None] * state + update, state)

    return lax.scan(advance, initial, (carry_factor, updates), reverse=backward)


def combine_states(earlier, later):
    return (earlier[0] * later[0], later[0][:, None, None] * earlier[1] + later[1])


def attend(weights, values, query_entry, state_low):
    near = jnp.einsum("bhts,bshd->bthd", widen(weights), widen(values))
    far = jnp.einsum("bthi,bhij->bthj", widen(query_entry), widen(state_low))
    return near + far


def gradients(
    query, keys, values, grad_blocks, weights, decay_mask, entry, leaving, state_low, grad_low
):
    raw = jnp.einsum("bthj,bshj->bhts", widen(grad_blocks), widen(values))
    masked = (raw * decay_mask).astype(jnp.bfloat16)
    query_part = jnp.einsum("bhts,bshi->bthi", widen(masked), widen(keys))
    query_part = query_part + entry[..., None] * jnp.einsum(
        "bthj,bhij->bthi", widen(grad_blocks), widen(state_low)
    )
    key_part = jnp.einsum("bhts,bthi->bshi", widen(masked), widen(query))
    key_part = key_part + leaving[..., None] * jnp.einsum(
        "bshj,bhij->bshi", widen(values), widen(grad_low)
    )
    value_part = jnp.einsum("bhts,bthj->bshj", widen(weights), widen(grad_blocks))
    value_part = value_part + leaving[..., None] * jnp.einsum(
        "bshi,bhij->bshj", widen(keys), widen(grad_low)
    )
    return (
        query_part.astype(jnp.bfloat16),
        key_part.astype(jnp.bfloat16),
        value_part.astype(jnp.bfloat16),
    )


def on_device(queries, keys_in, values_in, grad_output, log_decay, doc_lengths, norm_gain):
    tokens = queries.shape[1]
    features = queries.shape[2]
    heads = log_decay.shape[2]
    head_dim = features // heads
    nblk = tokens // BLK
    shape4 = (nblk, BLK, heads, head_dim)
    query = queries.reshape(shape4)
    keys = keys_in.reshape(shape4)
    values = values_in.reshape(shape4)
    positions = lax.axis_index("seq") * tokens + jnp.arange(tokens, dtype=jnp.int32)
    lengths = doc_lengths[0]
    starts = jnp.cumsum(lengths, dtype=jnp.int32) - lengths
    resets = jnp.any(positions[:, None] == starts[None, 1:], axis=1).reshape(nblk, BLK)
    entry, leaving, carry_factor, decay_mask = block_terms(log_decay, resets)
    weights, query_entry, block_state = forward_blocks(
        query, keys, values, entry, leaving, decay_mask
    )
    empty = jnp.zeros((heads, head_dim, head_dim), jnp.float32)
    local_state, _ = chain_states(carry_factor, block_state, empty, False)
    device_factor = jnp.prod(carry_factor, axis=0)
    identity = (jnp.ones_like(device_factor), empty)
    prefix = entering((device_factor, local_state), "seq", combine_states, identity, False)
    _, before = chain_states(carry_factor, block_state, prefix[1], False)
    state_low = before.astype(jnp.bfloat16)
    attn = attend(weights, values, query_entry, state_low).reshape(tokens, features)
    upstream = grad_output[0].astype(jnp.float32)
    scaled = upstream * norm_gain[None, :]
    squares = jnp.sum(attn * attn, axis=1)
    inner = jnp.sum(scaled * attn, axis=1)
    width = features * lax.axis_size("head")
    squares, inner = lax.psum((squares, inner), "head")
    recip = lax.rsqrt(squares / width + EPSILON)
    coef = recip * recip * recip * inner / width
    grad_attn = (recip[:, None] * scaled - coef[:, None] * attn).astype(jnp.bfloat16)
    gain_part = jnp.sum(upstream * attn * recip[:, None], axis=0)
    total_rows = tokens * lax.axis_size("seq") * lax.axis_size("dp")
    gain_grad = lax.psum(gain_part, ("seq", "dp")) / math.sqrt(total_rows)
    grad_blocks = grad_attn.reshape(shape4)
    grad_update = jnp.einsum("bthi,bthj->bhij", widen(query_entry), widen(grad_blocks))
    local_grad, _ = chain_states(carry_factor, grad_update, empty, True)
    suffix = entering((device_factor, local_grad), "seq", combine_states, identity, True)
    _, after = chain_states(carry_factor, grad_update, suffix[1], True)
    grad_low = after.astype(jnp.bfloat16)
    query_part, key_part, value_part = gradients(
        query, keys, values, grad_blocks, weights, decay_mask, entry, leaving, state_low, grad_low
    )
    out_shape = (1, tokens, features)
    return (
        query_part.reshape(out_shape),
        key_part.reshape(out_shape),
        value_part.reshape(out_shape),
        gain_grad,
    )


def solution(mesh):
    placed = (
        P("dp", "seq", "head"),
        P("dp", "seq", "head"),
        P("dp", "seq", "head"),
        P("dp", "seq", "head"),
        P("dp", "seq", "head"),
        P("dp", None),
        P("head"),
    )
    return jax.shard_map(
        on_device,
        mesh=mesh,
        in_specs=placed,
        out_specs=(
            P("dp", "seq", "head"),
            P("dp", "seq", "head"),
            P("dp", "seq", "head"),
            P("head"),
        ),
        check_vma=False,
    )
```

profile of v0, /device:TPU:2, one launch (start us, length us, event | category | flops | bytes accessed | tf_op | source)
XLA Modules:
  0.0 669.6 jit_solution(11159392049290616885)
XLA Ops:
  7.2 0.8 reduce-window.24
  8.1 0.7 bitcast_subtract_fusion
  9.7 0.6 slice.47
  10.2 0.6 compare_convert_fusion
  10.9 0.6 slice.46
  11.5 0.7 pad_bitcast_fusion
  12.2 0.6 reduce-window.32
  13.0 0.8 slice_reduce_fusion.1
  13.9 0.7 multiply_multiply_fusion.1
  14.5 1.1 copy.104
  15.7 1.3 copy.105
  17.1 1.6 convolution_add_fusion.2
  19.2 17.5 %all-gather = f32[16,1,8]{2,1,0:T(1,128)S(1)} all-gather(f32[1,1,8]{2,1,0:T(1,128)S(1)} %copy.78), channel_id=2, replica_groups=mesh['seq'=16,'head'=4,'dp'=16] {'seq'}, dimensions={0}, use_global_device_ids=true | all-gather | bytes 544 | tf_op jit(solution)/shard_map/all_gather | solution.py:16
  36.8 1.6 multiply_convert_fusion.1
  38.4 2.5 convolution_bitcast_fusion.6
  40.9 49.2 %all-gather.6.cloned.1.call-done = f32[128,128,128]{2,1,0:T(8,128)} async-done(((f32[8,128,128]{2,1,0:T(8,128)}), f32[128,128,128]{2,1,0:T(8,128)}) %all-gather.6.cloned.1.call-update) | async-done | bytes 8388624 | tf_op jit(solution)/shard_map/all_gather | solution.py:16
  90.1 18.2 %while.18 = (s32[]{:T(128)}, f32[8,128,128]{2,1,0:T(8,128)S(1)}, s32[]{:T(128)}, f32[16,8]{1,0:T(8,128)S(1)}, f32[16,8,128,128]{3,2,1,0:T(8,128)}, /*index=5*/s32[]{:T(128)}, s32[]{:T(128)}) while((s32[]{:T(128)}, f32[8,128,128]{2,1,0:T(8,128)S(1)}, s32[]{:T(128)}, f32[16,8]{1,0:T(8,128)S(1)}, f32[16,8,128,128]{3,2,1,0:T(8,128)}, ...), condition=%wide.region_7.8_spmd.clone, body=%wide.region_6.7_spmd.clone.sunk | while | flops 524292 | bytes 1573065 | solution.py:28
  90.1 1.2 fusion.47
  91.3 1.2 fusion.47
  92.5 1.2 fusion.47
  93.8 1.2 fusion.47
  95.0 1.2 fusion.47
  96.2 1.2 fusion.47
  97.4 1.2 fusion.47
  98.6 1.2 fusion.47
  99.8 1.2 fusion.47
  101.0 1.2 fusion.47
  102.3 1.2 fusion.47
  103.5 1.2 fusion.47
  104.7 1.2 fusion.47
  105.9 1.2 fusion.47
  107.1 1.2 fusion.47
  108.3 1.7 multiply_reduce_fusion.2
  110.0 8.6 %psum.21 = f32[224]{0:T(256)S(1)} all-reduce(f32[224]{0:T(256)S(1)} %get-tuple-element.353), channel_id=1, replica_groups=mesh['seq'=16,'head'=4,'dp'=16] {'head'}, use_global_device_ids=true, to_apply=%region_9.10 | all-reduce | flops 224 | bytes 1792 | tf_op jit(solution)/shard_map/psum | solution.py:138
  118.6 0.4 multiply_reduce_fusion
  119.0 10.1 %psum.22 = f32[224]{0:T(256)S(1)} all-reduce(f32[224]{0:T(256)S(1)} %get-tuple-element.325), channel_id=1, replica_groups=mesh['seq'=16,'head'=4,'dp'=16] {'head'}, use_global_device_ids=true, to_apply=%region_11.12 | all-reduce | flops 224 | bytes 1792 | tf_op jit(solution)/shard_map/psum | solution.py:138
  129.4 1.6 convolution_add_fusion.1
  131.2 0.6 multiply_convert_fusion
  131.9 0.4 copy-done.1
  132.3 0.4 convolution_bitcast_fusion.5
  133.2 0.9 copy.150
  134.1 495.4 %psum.23 = f32[1024]{0:T(1024)S(1)} all-reduce(f32[1024]{0:T(1024)S(1)} %bitcast.187), channel_id=1, replica_groups=mesh['seq'=16,'head'=4,'dp'=16] {'seq','dp'}, use_global_device_ids=true, to_apply=%region_15.16 | all-reduce | flops 1024 | bytes 8192 | tf_op jit(solution)/shard_map/psum | solution.py:144
  629.5 2.7 convolution_bitcast_fusion.3
  632.2 1.4 convolution_bitcast_fusion.4
  633.6 0.6 broadcast_multiply_fusion
  634.2 7.7 %rev.7 = f32[16,8,128,128]{3,2,1,0:T(8,128)} reverse(f32[16,8,128,128]{3,2,1,0:T(8,128)} %bitcast.163), dimensions={0} | reverse | bytes 16777216 | tf_op jit(solution)/shard_map/rev | solution.py:18
  641.9 18.3 %while.19 = (s32[]{:T(128)}, f32[8,128,128]{2,1,0:T(8,128)S(1)}, s32[]{:T(128)}, f32[16,8]{1,0:T(8,128)S(1)}, f32[16,8,128,128]{3,2,1,0:T(8,128)}, /*index=5*/s32[]{:T(128)}, s32[]{:T(128)}) while((s32[]{:T(128)}, f32[8,128,128]{2,1,0:T(8,128)S(1)}, s32[]{:T(128)}, f32[16,8]{1,0:T(8,128)S(1)}, f32[16,8,128,128]{3,2,1,0:T(8,128)}, ...), condition=%wide.region_13.14_spmd.clone, body=%wide.region_12.13_spmd.clone.sunk | while | flops 524292 | bytes 1573065 | solution.py:28
  642.0 1.3 fusion.48
  643.3 1.2 fusion.48
  644.5 1.2 fusion.48
  645.7 1.2 fusion.48
  646.9 1.2 fusion.48
  648.1 1.2 fusion.48
  649.3 1.2 fusion.48
  650.5 1.2 fusion.48
  651.8 1.2 fusion.48
  653.0 1.2 fusion.48
  654.2 1.2 fusion.48
  655.4 1.2 fusion.48
  656.6 1.2 fusion.48
  657.8 1.2 fusion.48
  659.0 1.2 fusion.48
  660.6 0.8 copy-done.4
  661.8 1.0 copy_bitcast_fusion
  (87 shorter events, 4.0 us)
Async XLA Ops:
  7.2 82.9 %all-gather.6.cloned.1.call-start = ((), (), s32[]{:S(2)}) async-start(), calls=%async_computation | async-start | bytes 8912896 | tf_op jit(solution)/shard_map/all_gather | solution.py:16
  14.5 4.3 copy-start.8
  15.7 21.1 %copy-start = (bf16[28,8,8,128]{3,2,1,0:T(8,128)(2,1)}, bf16[28,8,8,128]{3,2,1,0:T(8,128)(2,1)S(1)}, u32[]{:S(2)}) copy-start(bf16[28,8,8,128]{3,2,1,0:T(8,128)(2,1)S(1)} %copy.104) | copy-start | bytes 1376260
  15.7 3.2 copy-start.9
  17.0 21.4 %copy-start.2 = (bf16[28,8,8,128]{3,2,1,0:T(8,128)(2,1)}, bf16[28,8,8,128]{3,2,1,0:T(8,128)(2,1)S(1)}, u32[]{:S(2)}) copy-start(bf16[28,8,8,128]{3,2,1,0:T(8,128)(2,1)S(1)} %copy.105) | copy-start | bytes 1376260
  18.7 615.6 %all-gather.8.cloned.1.call-start = ((), (), s32[]{:S(2)}) async-start(), calls=%async_computation.1 | async-start | bytes 8912896 | tf_op jit(solution)/shard_map/all_gather | solution.py:16
  108.3 10.3 %copy-start.10 = (f32[1024]{0:T(1024)S(1)}, f32[1024]{0:T(1024)}, u32[]{:S(2)}) copy-start(f32[1024]{0:T(1024)} %param.17) | copy-start | bytes 12292
  129.4 1.8 copy-start.3
  131.2 1.0 copy-start.1
  132.3 0.9 copy-start.6
  629.5 2.7 copy-start.7
  641.9 18.3 %copy-start.5 = (f32[1,224,8,128]{3,1,2,0:T(8,128)S(1)}, f32[1,224,8,128]{3,1,2,0:T(8,128)}, u32[]{:S(2)}) copy-start(f32[1,224,8,128]{3,1,2,0:T(8,128)} %convolution_bitcast_fusion.4) | copy-start | bytes 2752516
  660.2 1.2 copy-start.4
Sparse Core Ops, SparseCore 0:
  18.8 71.2 all-gather.5
  131.1 61.7 all-gather.7
where the time goes:
time: 672 us; the launch traced here: 670 us
  blocking collectives  532 us (79%)
  waiting for transfers between devices  49.3 us (7%)
  other arithmetic  41.7 us (6%)
  local copies, waits for them, and re-layouts  16.7 us (2%)
  matrix products  15.1 us (2%)
  between operations  14.3 us (2%)
    psum x1, blocking collectives, on_device(): gain_grad = lax.psum(gain_part, ('seq', 'dp')) / math.sqrt(total_rows)  495 us
    all_gather x2, waiting for transfers between devices, entering(): pieces = jax.tree.map(lambda part: lax.all_gather(part, axis), value)  49.2 us
    select_n x30, other arithmetic, turn(): jnp.where(position < mine, new, old)  35.3 us
    psum x2, blocking collectives, on_device(): squares, inner = lax.psum((squares, inner), 'head')  18.7 us
    all_gather x1, blocking collectives, entering(): pieces = jax.tree.map(lambda part: lax.all_gather(part, axis), value)  17.5 us
  transfers between devices with their start and end apart: 2, of which 1 were waited for; matrix products, arithmetic and copies ran while one was open for 2% of the time, Pallas kernels for 0%

commit v1 on v0

v1 whole, which is shorter than its diff:
```python
import functools
import math

import jax
import jax.numpy as jnp
from jax import lax
from jax.experimental import pallas as pl
from jax.experimental.pallas import tpu as pltpu
from jax.sharding import PartitionSpec as P

EPSILON = 1e-06
HD = 128
TAG = 8
SPLIT = 2
UNROLL = 2
MESH = pl.DeviceIdType.MESH
EXACT = lax.Precision.HIGHEST
F32 = jnp.float32
BF16 = jnp.bfloat16


def dot(left, right, over_left, over_right, precision=None):
    return lax.dot_general(
        left,
        right,
        (((over_left,), (over_right,)), ((), ())),
        preferred_element_type=F32,
        precision=precision,
    )


def each_head(body, start, count):
    def turn(step, carried):
        body([start + step * UNROLL + one for one in range(UNROLL)])
        return carried

    lax.fori_loop(0, count // UNROLL, turn, 0)


def kernel(
    seqs,
    teams,
    q_hbm,
    k_hbm,
    v_hbm,
    up_hbm,
    log_hbm,
    lengths,
    gain_in,
    q_out,
    k_out,
    v_out,
    gain_out,
    q_ref,
    k_ref,
    v_ref,
    up_ref,
    log_ref,
    c_row,
    c_col,
    bias_ref,
    enter_ref,
    leave_ref,
    decay_ref,
    weight_ref,
    entered_ref,
    attn_ref,
    grad_ref,
    squares_ref,
    inner_ref,
    k_part,
    v_part,
    own_ref,
    peer_ref,
    chain_in,
    chain_out,
    pass_ref,
    far_ref,
    state_ref,
    sums_ref,
    sums_in,
    load_sem,
    pair_send,
    pair_recv,
    chain_send,
    chain_recv,
    pass_send,
    pass_recv,
    sums_send,
    sums_recv,
):
    blk, features = q_ref.shape
    heads = features // HD
    half = heads // 2
    chunks = half * SPLIT
    span = HD // SPLIT
    chips = seqs // 2
    seq = lax.axis_index("seq")
    team = lax.axis_index("head")
    core = lax.rem(seq, 2)
    chip = lax.div(seq, 2)
    other = 1 - core
    peer = seq + 1 - 2 * core

    loads = [
        pltpu.make_async_copy(source.at[0], target, load_sem.at[slot])
        for slot, (source, target) in enumerate(
            [(log_hbm, log_ref), (k_hbm, k_ref), (v_hbm, v_ref), (q_hbm, q_ref), (up_hbm, up_ref)]
        )
    ]
    for load in loads:
        load.start()

    barrier = pltpu.get_barrier_semaphore()
    pl.semaphore_signal(barrier, inc=1, device_id={"seq": peer}, device_id_type=MESH)
    for step in range(1, teams):
        pl.semaphore_signal(
            barrier, inc=1, device_id={"head": lax.rem(team + step, teams)}, device_id_type=MESH
        )

    @pl.when(chip > 0)
    def _():
        pl.semaphore_signal(barrier, inc=1, device_id={"seq": seq - 2}, device_id_type=MESH)

    @pl.when(chip < chips - 1)
    def _():
        pl.semaphore_signal(barrier, inc=1, device_id={"seq": seq + 2}, device_id_type=MESH)

    def lanes(head):
        return pl.ds(pl.multiple_of(head * HD, HD), HD)

    row = lax.broadcasted_iota(jnp.int32, (blk, blk), 0)
    col = lax.broadcasted_iota(jnp.int32, (blk, blk), 1)
    triangle = (col <= row).astype(F32)
    places = []
    total = 0
    for one in range(lengths.shape[1] - 1):
        total = total + lengths[0, one]
        place = total - seq * blk
        places.append(jnp.where(place < 0, 2 * blk, place))
    at_row = lax.broadcasted_iota(jnp.int32, (blk, 1), 0)
    at_col = lax.broadcasted_iota(jnp.int32, (1, blk), 1)
    z_row = sum((at_row >= place).astype(jnp.int32) for place in places)
    z_col = sum((at_col >= place).astype(jnp.int32) for place in places)
    z_end = sum(jnp.where(place < blk, 1, 0) for place in places)
    loads[0].wait()
    log = log_ref[...]
    c_all = dot(triangle, log, 1, 1, EXACT)
    tail = c_all[blk - 1 : blk, :]
    leaving = jnp.exp(tail - c_all) * (z_row == z_end).astype(F32)
    carry = jnp.exp(tail) * jnp.where(z_end == 0, 1.0, 0.0)
    for head in range(heads):
        leave_ref[head] = jnp.broadcast_to(leaving[:, head : head + 1], (blk, HD))
        tag = jnp.broadcast_to(carry[:, head : head + 1], (TAG, HD))
        own_ref[0, head, HD : HD + TAG, :] = tag
        own_ref[1, head, HD : HD + TAG, :] = tag

    def block_state(group):
        made = []
        for head in group:
            left = (k_ref[:, lanes(head)].astype(F32) * leave_ref[head]).astype(BF16)
            made.append(dot(left, v_ref[:, lanes(head)], 0, 0))
        for head, value in zip(group, made):
            own_ref[0, head, 0:HD, :] = value

    def exchange(way):
        return pltpu.make_async_remote_copy(
            src_ref=own_ref.at[way, pl.ds(other * half, half)],
            dst_ref=peer_ref.at[way],
            send_sem=pair_send.at[way],
            recv_sem=pair_recv.at[way],
            device_id={"seq": peer},
            device_id_type=MESH,
        )

    def ahead(way, index, to):
        at = (way, lax.div(index, SPLIT), pl.ds(pl.multiple_of(lax.rem(index, SPLIT) * span, span), span))
        return pltpu.make_async_remote_copy(
            src_ref=chain_out.at[at],
            dst_ref=chain_in.at[at],
            send_sem=chain_send.at[way, index],
            recv_sem=chain_recv.at[way, index],
            device_id={"seq": to},
            device_id_type=MESH,
        )

    def across(way, index):
        at = (way, lax.div(index, SPLIT), pl.ds(pl.multiple_of(lax.rem(index, SPLIT) * span, span), span))
        return pltpu.make_async_remote_copy(
            src_ref=pass_ref.at[at],
            dst_ref=far_ref.at[at],
            send_sem=pass_send.at[way, index],
            recv_sem=pass_recv.at[way, index],
            device_id={"seq": peer},
            device_id_type=MESH,
        )

    def chain(way, first, has_prev, has_next, to):
        exchange(way).wait_recv()

        def joined(local, carried):
            mine = own_ref[way, core * half + local, 0:HD, :]
            theirs = peer_ref[way, local, 0:HD, :]
            my_carry = own_ref[way, core * half + local, HD : HD + 1, :]
            their_carry = peer_ref[way, local, HD : HD + 1, :]
            chain_out[way, local] = jnp.where(
                first, their_carry * mine + theirs, my_carry * theirs + mine
            )
            return carried

        @pl.when(has_next)
        def _():
            lax.fori_loop(0, half, joined, 0)

        @pl.when(jnp.logical_not(has_prev))
        def _():
            chain_in[way] = jnp.zeros(chain_in.shape[1:], F32)

        def turn(index, carried):
            local = lax.div(index, SPLIT)
            rows = pl.ds(pl.multiple_of(lax.rem(index, SPLIT) * span, span), span)
            my_carry = own_ref[way, core * half + local, HD : HD + 1, :]
            their_carry = peer_ref[way, local, HD : HD + 1, :]

            @pl.when(has_prev)
            def _():
                ahead(way, index, to).wait_recv()

            state = chain_in[way, local, rows, :]

            @pl.when(has_next)
            def _():
                chain_out[way, local, rows, :] = (
                    my_carry * their_carry * state + chain_out[way, local, rows, :]
                )
                ahead(way, index, to).start()

            mine = own_ref[way, core * half + local, rows, :]
            theirs = peer_ref[way, local, rows, :]
            middle = jnp.where(first, my_carry * state + mine, their_carry * state + theirs)
            pass_ref[way, local, rows, :] = jnp.where(first, middle, state)
            across(way, index).start()
            state_ref[way, core * half + local, rows, :] = jnp.where(first, state, middle).astype(BF16)
            return carried

        lax.fori_loop(0, chunks, turn, 0)

        def land(index, carried):
            local = lax.div(index, SPLIT)
            rows = pl.ds(pl.multiple_of(lax.rem(index, SPLIT) * span, span), span)
            across(way, index).wait_recv()
            state_ref[way, other * half + local, rows, :] = far_ref[way, local, rows, :].astype(BF16)
            return carried

        lax.fori_loop(0, chunks, land, 0)

    loads[1].wait()
    loads[2].wait()
    each_head(block_state, other * half, half)
    pl.semaphore_wait(
        barrier, teams + jnp.where(chip > 0, 1, 0) + jnp.where(chip < chips - 1, 1, 0)
    )
    exchange(0).start()
    each_head(block_state, core * half, half)

    c_row[...] = dot(log, triangle, 1, 1, EXACT)
    entering = jnp.exp(c_all) * (z_row == 0).astype(F32)
    for head in range(heads):
        enter_ref[head] = jnp.broadcast_to(entering[:, head : head + 1], (blk, HD))
        c_col[head] = jnp.broadcast_to(c_all[:, head : head + 1], (blk, HD))
    bias_ref[...] = jnp.where((z_row == z_col) & (col <= row), 0.0, -1e30)
    loads[3].wait()
    loads[4].wait()

    def near(group):
        made = []
        for head in group:
            query = q_ref[:, lanes(head)]
            scores = dot(query, k_ref[:, lanes(head)], 1, 1)
            start = jnp.broadcast_to(c_col[head][:, 0:1], (blk, blk))
            decay = jnp.exp(start - c_row[pl.ds(head, 1), :] + bias_ref[...])
            weight = (scores * decay).astype(BF16)
            entered = (query.astype(F32) * enter_ref[head]).astype(BF16)
            made.append((decay, weight, entered, dot(weight, v_ref[:, lanes(head)], 1, 0)))
        for head, (decay, weight, entered, value) in zip(group, made):
            decay_ref[head] = decay
            weight_ref[head] = weight
            entered_ref[head] = entered
            attn_ref[head] = value

    early = chips // 2 - 1

    @pl.when(chip >= early)
    def _():
        each_head(near, 0, heads)

    chain(0, core == 0, chip > 0, chip < chips - 1, lax.rem(seq + 2, seqs))

    @pl.when(chip < early)
    def _():
        each_head(near, 0, heads)

    squares_ref[...] = jnp.zeros_like(squares_ref)
    inner_ref[...] = jnp.zeros_like(inner_ref)

    def attend(group):
        squares, inner = squares_ref[...], inner_ref[...]
        made = []
        for head in group:
            attn = attn_ref[head] + dot(entered_ref[head], state_ref[0, head], 1, 0)
            scaled = up_ref[:, lanes(head)].astype(F32) * gain_in[pl.ds(head, 1), :]
            squares = squares + attn * attn
            inner = inner + scaled * attn
            made.append(attn)
        for head, attn in zip(group, made):
            attn_ref[head] = attn
        squares_ref[...] = squares
        inner_ref[...] = inner

    each_head(attend, 0, heads)
    ones = jnp.ones((8, HD), F32)
    sums_ref[0:8, :] = dot(ones, squares_ref[...], 1, 1, EXACT)
    sums_ref[8:16, :] = dot(ones, inner_ref[...], 1, 1, EXACT)
    shares = [
        pltpu.make_async_remote_copy(
            src_ref=sums_ref,
            dst_ref=sums_in.at[step - 1],
            send_sem=sums_send.at[step - 1],
            recv_sem=sums_recv.at[step - 1],
            device_id={"head": lax.rem(team + step, teams)},
            device_id_type=MESH,
        )
        for step in range(1, teams)
    ]
    for share in shares:
        share.start()
    for share in shares:
        share.wait_recv()
    sums = sums_ref[...]
    for step in range(1, teams):
        sums = sums + sums_in[step - 1]
    width = features * teams
    chosen = lax.broadcasted_iota(jnp.int32, (8, HD), 0)
    chosen = jnp.where(chosen == 0, 1.0, 0.0).astype(F32)
    squares = dot(sums[0:8, :], chosen, 0, 0, EXACT)
    inner = dot(sums[8:16, :], chosen, 0, 0, EXACT)
    recip = lax.rsqrt(squares / width + EPSILON)
    squares_ref[...] = recip
    inner_ref[...] = recip * recip * recip * inner / width

    def gradient(group):
        recip, coef = squares_ref[...], inner_ref[...]
        made = []
        for head in group:
            attn = attn_ref[head]
            upstream = up_ref[:, lanes(head)].astype(F32)
            scaled = upstream * gain_in[pl.ds(head, 1), :]
            grad = (recip * scaled - coef * attn).astype(BF16)
            part = jnp.sum(upstream * attn * recip, axis=0, keepdims=True)
            made.append((grad, part, dot(entered_ref[head], grad, 0, 0)))
        for head, (grad, part, value) in zip(group, made):
            grad_ref[head] = grad
            gain_out[pl.ds(head, 1), :] = part
            own_ref[1, head, 0:HD, :] = value

    each_head(gradient, other * half, half)
    exchange(1).start()
    each_head(gradient, core * half, half)

    def masked(group):
        made = []
        for head in group:
            grad = grad_ref[head]
            raw = dot(grad, v_ref[:, lanes(head)], 1, 1)
            mask = (raw * decay_ref[head]).astype(BF16)
            query = dot(mask, k_ref[:, lanes(head)], 1, 0)
            query = query + enter_ref[head] * dot(grad, state_ref[0, head], 1, 1)
            made.append(
                (
                    query.astype(BF16),
                    dot(mask, q_ref[:, lanes(head)], 0, 0),
                    dot(weight_ref[head], grad, 0, 0),
                )
            )
        for head, (query, key, value) in zip(group, made):
            q_out[0, :, lanes(head)] = query
            k_part[head] = key
            v_part[head] = value

    late = chips - early

    @pl.when(chip < late)
    def _():
        each_head(masked, 0, heads)

    chain(1, core == 1, chip < chips - 1, chip > 0, lax.rem(seq + seqs - 2, seqs))

    @pl.when(chip >= late)
    def _():
        each_head(masked, 0, heads)

    def finish(group):
        made = []
        for head in group:
            state = state_ref[1, head]
            leave = leave_ref[head]
            key = k_part[head] + leave * dot(v_ref[:, lanes(head)], state, 1, 1)
            value = v_part[head] + leave * dot(k_ref[:, lanes(head)], state, 1, 0)
            made.append((key.astype(BF16), value.astype(BF16)))
        for head, (key, value) in zip(group, made):
            k_out[0, :, lanes(head)] = key
            v_out[0, :, lanes(head)] = value

    each_head(finish, 0, heads)

    for share in shares:
        share.wait_send()
    for way, has_next in ((0, chip < chips - 1), (1, chip > 0)):
        exchange(way).wait_send()

        def sent(index, carried, way=way, has_next=has_next):
            @pl.when(has_next)
            def _():
                ahead(way, index, peer).wait_send()

            across(way, index).wait_send()
            return carried

        lax.fori_loop(0, chunks, sent, 0)


def on_device(seqs, teams, queries, keys_in, values_in, grad_output, log_decay, lengths, norm_gain):
    tokens, features = queries.shape[1:]
    heads = log_decay.shape[2]
    half = heads // 2
    chunks = half * SPLIT
    whole = jax.ShapeDtypeStruct((1, tokens, features), BF16)
    anywhere = pl.BlockSpec(memory_space=pltpu.HBM)
    vmem = pl.BlockSpec(memory_space=pltpu.VMEM)
    wide = pltpu.VMEM((heads, tokens, HD), F32)
    states = pltpu.VMEM((2, half, HD, HD), F32)
    query_grad, key_grad, value_grad, gain = pl.pallas_call(
        functools.partial(kernel, seqs, teams),
        out_shape=(whole, whole, whole, jax.ShapeDtypeStruct((heads, HD), F32)),
        in_specs=[anywhere] * 5 + [pl.BlockSpec(memory_space=pltpu.SMEM), vmem],
        out_specs=[vmem] * 4,
        scratch_shapes=[
            pltpu.VMEM((tokens, features), BF16),
            pltpu.VMEM((tokens, features), BF16),
            pltpu.VMEM((tokens, features), BF16),
            pltpu.VMEM((tokens, features), BF16),
            pltpu.VMEM((heads, tokens), F32),
            pltpu.VMEM((heads, tokens), F32),
            wide,
            pltpu.VMEM((tokens, tokens), F32),
            wide,
            wide,
            pltpu.VMEM((heads, tokens, tokens), F32),
            pltpu.VMEM((heads, tokens, tokens), BF16),
            pltpu.VMEM((heads, tokens, HD), BF16),
            wide,
            pltpu.VMEM((heads, tokens, HD), BF16),
            pltpu.VMEM((tokens, HD), F32),
            pltpu.VMEM((tokens, HD), F32),
            wide,
            wide,
            pltpu.VMEM((2, heads, HD + TAG, HD), F32),
            pltpu.VMEM((2, half, HD + TAG, HD), F32),
            states,
            states,
            states,
            states,
            pltpu.VMEM((2, heads, HD, HD), BF16),
            pltpu.VMEM((16, tokens), F32),
            pltpu.VMEM((teams - 1, 16, tokens), F32),
            pltpu.SemaphoreType.DMA((5,)),
            pltpu.SemaphoreType.DMA((2,)),
            pltpu.SemaphoreType.DMA((2,)),
            pltpu.SemaphoreType.DMA((2, chunks)),
            pltpu.SemaphoreType.DMA((2, chunks)),
            pltpu.SemaphoreType.DMA((2, chunks)),
            pltpu.SemaphoreType.DMA((2, chunks)),
            pltpu.SemaphoreType.DMA((teams - 1,)),
            pltpu.SemaphoreType.DMA((teams - 1,)),
        ],
        compiler_params=pltpu.CompilerParams(
            collective_id=0, has_side_effects=True, vmem_limit_bytes=48 * 1024 * 1024
        ),
    )(
        queries,
        keys_in,
        values_in,
        grad_output,
        jnp.swapaxes(log_decay, 1, 2),
        lengths,
        norm_gain.reshape(heads, HD),
    )
    rows = tokens * seqs * lax.axis_size("dp")
    gain_grad = lax.psum(gain.reshape(features), ("seq", "dp")) / math.sqrt(rows)
    return query_grad, key_grad, value_grad, gain_grad


def solution(mesh):
    split = P("dp", "seq", "head")
    return jax.shard_map(
        functools.partial(on_device, mesh.shape["seq"], mesh.shape["head"]),
        mesh=mesh,
        in_specs=(split, split, split, split, split, P("dp", None), P("head")),
        out_specs=(split, split, split, P("head")),
        check_vma=False,
    )
```

time: 672 us -> 581 us (0.86)
  the two profiles are of different devices: /device:TPU:2 before, /device:TPU:64 now
where the time goes in v1:
time: 581 us
  blocking collectives  504 us (87%)
  Pallas kernels  67.4 us (12%)
  local copies, waits for them, and re-layouts  8.4 us (1%)
    psum x1, blocking collectives, on_device(): lax.psum(gain.reshape(features), ('seq', 'dp')) / math.sqrt(rows)  504 us
    pallas_call x1, Pallas kernels, on_device(): pl.pallas_call(functools.partial(kernel, seqs, teams), out_shape=(whole,...  67.4 us

profile of v1, /device:TPU:64, one launch (start us, length us, event | category | flops | bytes accessed | tf_op | source)
XLA Modules:
  0.0 580.9 jit_solution(15746410820857737720)
XLA Ops:
  0.6 0.0 copy-start.6
  0.6 0.6 copy-done.6
  1.3 0.0 copy-start
  1.3 1.0 copy-done
  2.3 0.0 copy-start.1
  2.3 1.0 copy-done.1
  3.3 0.0 copy-start.2
  3.3 1.0 copy-done.2
  4.3 0.0 copy-start.3
  4.3 1.0 copy-done.3
  5.4 0.0 copy-start.4
  5.4 0.7 copy-done.4
  6.1 0.0 copy-start.5
  6.1 0.7 copy-done.5
  6.8 67.4 %shard_map.102 = (bf16[1,224,1024]{2,1,0:T(8,128)(2,1)S(1)}, bf16[1,224,1024]{2,1,0:T(8,128)(2,1)S(1)}, bf16[1,224,1024]{2,1,0:T(8,128)(2,1)S(1)}, f32[8,128]{1,0:T(8,128)S(1)}) custom-call(bf16[1,224,1024]{2,1,0:T(8,128)(2,1)S(1)} %copy-done, bf16[1,224,1024]{2,1,0:T(8,128)(2,1)S(1)} %copy-done.1, bf16[1,224,1024]{2,1,0:T(8,128)(2,1)S(1)} %copy-done.2, ...), custom_call_target="tpu_custom_call" | custom-call | tf_op jit(solution)/shard_map/pallas_call | solution.py:442
  74.2 503.8 %psum.7 = f32[1024]{0:T(1024)S(1)} all-reduce(f32[1024]{0:T(1024)S(1)} %bitcast.5), channel_id=1, replica_groups=mesh['seq'=16,'head'=4,'dp'=16] {'seq','dp'}, use_global_device_ids=true, to_apply=%region_0.0 | all-reduce | flops 1024 | bytes 8192 | tf_op jit(solution)/shard_map/psum | solution.py:499
  578.0 0.6 broadcast_multiply_fusion
  578.6 0.8 copy.14
  579.4 0.8 copy.15
  580.2 0.8 copy.16
Async XLA Ops:
  0.6 0.7 copy-start.6
  1.3 1.0 copy-start
  2.3 1.0 copy-start.1
  3.3 1.0 copy-start.2
  4.3 1.0 copy-start.3
  5.4 0.7 copy-start.4
  6.1 0.7 copy-start.5

commit v2 on v1

--- a/solution.py
+++ b/solution.py
@@ -40,6 +40,7 @@
 def kernel(
     seqs,
     teams,
+    rows_of,
     q_hbm,
     k_hbm,
     v_hbm,
@@ -79,6 +80,10 @@
     state_ref,
     sums_ref,
     sums_in,
+    gain_row,
+    gain_chips,
+    gain_rows,
+    gain_far,
     load_sem,
     pair_send,
     pair_recv,
@@ -88,6 +93,11 @@
     pass_recv,
     sums_send,
     sums_recv,
+    gain_chips_send,
+    gain_chips_recv,
+    gain_rows_send,
+    gain_rows_recv,
+    gain_far_sem,
 ):
     blk, features = q_ref.shape
     heads = features // HD
@@ -97,6 +107,7 @@
     chips = seqs // 2
     seq = lax.axis_index("seq")
     team = lax.axis_index("head")
+    place_z = lax.axis_index("dp")
     core = lax.rem(seq, 2)
     chip = lax.div(seq, 2)
     other = 1 - core
@@ -118,13 +129,18 @@
             barrier, inc=1, device_id={"head": lax.rem(team + step, teams)}, device_id_type=MESH
         )
 
-    @pl.when(chip > 0)
-    def _():
-        pl.semaphore_signal(barrier, inc=1, device_id={"seq": seq - 2}, device_id_type=MESH)
-
-    @pl.when(chip < chips - 1)
-    def _():
-        pl.semaphore_signal(barrier, inc=1, device_id={"seq": seq + 2}, device_id_type=MESH)
+    for step in range(1, chips):
+        pl.semaphore_signal(
+            barrier, inc=1, device_id={"seq": lax.rem(seq + 2 * step, seqs)}, device_id_type=MESH
+        )
+
+    def greet(step, carried):
+        pl.semaphore_signal(
+            barrier, inc=1, device_id={"dp": lax.rem(place_z + step, rows_of)}, device_id_type=MESH
+        )
+        return carried
+
+    lax.fori_loop(1, rows_of, greet, 0)
 
     def lanes(head):
         return pl.ds(pl.multiple_of(head * HD, HD), HD)
@@ -195,7 +211,7 @@
             device_id_type=MESH,
         )
 
-    def chain(way, first, has_prev, has_next, to):
+    def join(way, first, has_next):
         exchange(way).wait_recv()
 
         def joined(local, carried):
@@ -212,6 +228,7 @@
         def _():
             lax.fori_loop(0, half, joined, 0)
 
+    def chain(way, first, has_prev, has_next, to):
         @pl.when(jnp.logical_not(has_prev))
         def _():
             chain_in[way] = jnp.zeros(chain_in.shape[1:], F32)
@@ -257,9 +274,7 @@
     loads[1].wait()
     loads[2].wait()
     each_head(block_state, other * half, half)
-    pl.semaphore_wait(
-        barrier, teams + jnp.where(chip > 0, 1, 0) + jnp.where(chip < chips - 1, 1, 0)
-    )
+    pl.semaphore_wait(barrier, 1 + teams - 1 + chips - 1 + rows_of - 1)
     exchange(0).start()
     each_head(block_state, core * half, half)
 
@@ -294,6 +309,7 @@
     def _():
         each_head(near, 0, heads)
 
+    join(0, core == 0, chip < chips - 1)
     chain(0, core == 0, chip > 0, chip < chips - 1, lax.rem(seq + 2, seqs))
 
     @pl.when(chip < early)
@@ -360,7 +376,8 @@
             made.append((grad, part, dot(entered_ref[head], grad, 0, 0)))
         for head, (grad, part, value) in zip(group, made):
             grad_ref[head] = grad
-            gain_out[pl.ds(head, 1), :] = part
+            gain_row[pl.ds(head, 1), :] = part
+            own_ref[1, head, HD + 1 : HD + 2, :] = part
             own_ref[1, head, 0:HD, :] = value
 
     each_head(gradient, other * half, half)
@@ -387,17 +404,112 @@
             k_part[head] = key
             v_part[head] = value
 
+    def over_chips(step):
+        to = lax.rem(chip + step, chips)
+        return pltpu.make_async_remote_copy(
+            src_ref=gain_chips.at[chip],
+            dst_ref=gain_chips.at[chip],
+            send_sem=gain_chips_send.at[step - 1],
+            recv_sem=gain_chips_recv.at[chip],
+            device_id={"seq": 2 * to + core},
+            device_id_type=MESH,
+        )
+
+    def from_chips(step):
+        place = lax.rem(chip + step, chips)
+        return pltpu.make_async_remote_copy(
+            src_ref=gain_chips.at[place],
+            dst_ref=gain_chips.at[place],
+            send_sem=gain_chips_send.at[step - 1],
+            recv_sem=gain_chips_recv.at[place],
+            device_id={"seq": 2 * place + core},
+            device_id_type=MESH,
+        )
+
+    def over_rows(step):
+        return pltpu.make_async_remote_copy(
+            src_ref=gain_rows.at[place_z],
+            dst_ref=gain_rows.at[place_z],
+            send_sem=gain_rows_send.at[step - 1],
+            recv_sem=gain_rows_recv.at[place_z],
+            device_id={"dp": lax.rem(place_z + step, rows_of)},
+            device_id_type=MESH,
+        )
+
+    def from_rows(step):
+        place = lax.rem(place_z + step, rows_of)
+        return pltpu.make_async_remote_copy(
+            src_ref=gain_rows.at[place],
+            dst_ref=gain_rows.at[place],
+            send_sem=gain_rows_send.at[step - 1],
+            recv_sem=gain_rows_recv.at[place],
+            device_id={"dp": place},
+            device_id_type=MESH,
+        )
+
+    def each_step(stop, action):
+        def turn(step, carried):
+            action(step)
+            return carried
+
+        lax.fori_loop(1, stop, turn, 0)
+
+    def gain_begin():
+        for local in range(half):
+            gain_chips[chip, local : local + 1, :] = (
+                gain_row[pl.ds(core * half + local, 1), :] + peer_ref[1, local, HD + 1 : HD + 2, :]
+            )
+        each_step(chips, lambda step: over_chips(step).start())
+
+    def gain_middle():
+        each_step(chips, lambda step: from_chips(step).wait_recv())
+        total = gain_chips[0]
+        for one in range(1, chips):
+            total = total + gain_chips[one]
+        gain_rows[place_z] = total
+        each_step(rows_of, lambda step: over_rows(step).start())
+
+    gain_pass = pltpu.make_async_remote_copy(
+        src_ref=gain_far.at[0],
+        dst_ref=gain_far.at[1],
+        send_sem=gain_far_sem.at[0],
+        recv_sem=gain_far_sem.at[1],
+        device_id={"seq": peer},
+        device_id_type=MESH,
+    )
+
+    def gain_end():
+        each_step(rows_of, lambda step: from_rows(step).wait_recv())
+        total = gain_rows[0]
+        for one in range(1, rows_of):
+            total = total + gain_rows[one]
+        gain_far[0] = total / math.sqrt(blk * seqs * rows_of)
+        gain_pass.start()
+
     late = chips - early
+    back = (core == 1, chip < chips - 1, chip > 0, lax.rem(seq + seqs - 2, seqs))
 
     @pl.when(chip < late)
     def _():
-        each_head(masked, 0, heads)
-
-    chain(1, core == 1, chip < chips - 1, chip > 0, lax.rem(seq + seqs - 2, seqs))
+        each_head(masked, 0, half)
+        join(1, core == 1, chip > 0)
+        gain_begin()
+        each_head(masked, half, half)
+        gain_middle()
+
+    @pl.when(chip >= late)
+    def _():
+        join(1, core == 1, chip > 0)
+        gain_begin()
+
+    chain(1, *back)
 
     @pl.when(chip >= late)
     def _():
         each_head(masked, 0, heads)
+        gain_middle()
+
+    gain_end()
 
     def finish(group):
         made = []
@@ -413,6 +525,13 @@
 
     each_head(finish, 0, heads)
 
+    gain_pass.wait_recv()
+    for local in range(half):
+        gain_out[pl.ds(core * half + local, 1), :] = gain_far[0, local : local + 1, :]
+        gain_out[pl.ds(other * half + local, 1), :] = gain_far[1, local : local + 1, :]
+    gain_pass.wait_send()
+    each_step(chips, lambda step: over_chips(step).wait_send())
+    each_step(rows_of, lambda step: over_rows(step).wait_send())
     for share in shares:
         share.wait_send()
     for way, has_next in ((0, chip < chips - 1), (1, chip > 0)):
@@ -429,7 +548,7 @@
         lax.fori_loop(0, chunks, sent, 0)
 
 
-def on_device(seqs, teams, queries, keys_in, values_in, grad_output, log_decay, lengths, norm_gain):
+def on_device(seqs, teams, rows_of, queries, keys_in, values_in, grad_output, log_decay, lengths, norm_gain):
     tokens, features = queries.shape[1:]
     heads = log_decay.shape[2]
     half = heads // 2
@@ -440,7 +559,7 @@
     wide = pltpu.VMEM((heads, tokens, HD), F32)
     states = pltpu.VMEM((2, half, HD, HD), F32)
     query_grad, key_grad, value_grad, gain = pl.pallas_call(
-        functools.partial(kernel, seqs, teams),
+        functools.partial(kernel, seqs, teams, rows_of),
         out_shape=(whole, whole, whole, jax.ShapeDtypeStruct((heads, HD), F32)),
         in_specs=[anywhere] * 5 + [pl.BlockSpec(memory_space=pltpu.SMEM), vmem],
         out_specs=[vmem] * 4,
@@ -473,6 +592,10 @@
             pltpu.VMEM((2, heads, HD, HD), BF16),
             pltpu.VMEM((16, tokens), F32),
             pltpu.VMEM((teams - 1, 16, tokens), F32),
+            pltpu.VMEM((heads, HD), F32),
+            pltpu.VMEM((seqs // 2, half, HD), F32),
+            pltpu.VMEM((rows_of, half, HD), F32),
+            pltpu.VMEM((2, half, HD), F32),
             pltpu.SemaphoreType.DMA((5,)),
             pltpu.SemaphoreType.DMA((2,)),
             pltpu.SemaphoreType.DMA((2,)),
@@ -482,9 +605,14 @@
             pltpu.SemaphoreType.DMA((2, chunks)),
             pltpu.SemaphoreType.DMA((teams - 1,)),
             pltpu.SemaphoreType.DMA((teams - 1,)),
+            pltpu.SemaphoreType.DMA((seqs // 2 - 1,)),
+            pltpu.SemaphoreType.DMA((seqs // 2,)),
+            pltpu.SemaphoreType.DMA((rows_of - 1,)),
+            pltpu.SemaphoreType.DMA((rows_of,)),
+            pltpu.SemaphoreType.DMA((2,)),
         ],
         compiler_params=pltpu.CompilerParams(
-            collective_id=0, has_side_effects=True, vmem_limit_bytes=48 * 1024 * 1024
+            collective_id=0, has_side_effects=True, vmem_limit_bytes=63 * 1024 * 1024
         ),
     )(
         queries,
@@ -495,15 +623,13 @@
         lengths,
         norm_gain.reshape(heads, HD),
     )
-    rows = tokens * seqs * lax.axis_size("dp")
-    gain_grad = lax.psum(gain.reshape(features), ("seq", "dp")) / math.sqrt(rows)
-    return query_grad, key_grad, value_grad, gain_grad
+    return query_grad, key_grad, value_grad, gain.reshape(features)
 
 
 def solution(mesh):
     split = P("dp", "seq", "head")
     return jax.shard_map(
-        functools.partial(on_device, mesh.shape["seq"], mesh.shape["head"]),
+        functools.partial(on_device, mesh.shape["seq"], mesh.shape["head"], mesh.shape["dp"]),
         mesh=mesh,
         in_specs=(split, split, split, split, split, P("dp", None), P("head")),
         out_specs=(split, split, split, P("head")),

time: 581 us -> 92 us (0.16)
  the two profiles are of different devices: /device:TPU:64 before, /device:TPU:1 now
where the time goes in v2:
time: 92 us; the launch traced here: 91.7 us
  Pallas kernels  86.7 us (94%)
  local copies, waits for them, and re-layouts  4.42 us (5%)
    pallas_call x1, Pallas kernels, on_device(): pl.pallas_call(functools.partial(kernel, seqs, teams, rows_of), out_shape...  86.7 us
    unnamed x10, local copies, waits for them, and re-layouts  4.42 us

profile of v2, /device:TPU:1, one launch (start us, length us, event | category | flops | bytes accessed | tf_op | source)
XLA Modules:
  0.0 91.7 jit_solution(2568143219710804901)
XLA Ops:
  0.6 86.7 %shard_map.102 = (bf16[1,224,1024]{2,1,0:T(8,128)(2,1)}, bf16[1,224,1024]{2,1,0:T(8,128)(2,1)}, bf16[1,224,1024]{2,1,0:T(8,128)(2,1)}, f32[8,128]{1,0:T(8,128)}) custom-call(bf16[1,224,1024]{2,1,0:T(8,128)(2,1)} %q_hbm.1, bf16[1,224,1024]{2,1,0:T(8,128)(2,1)} %k_hbm.1, bf16[1,224,1024]{2,1,0:T(8,128)(2,1)} %v_hbm.1, bf16[1,224,1024]{2,1,0:T(8,128)(2,1)} %up_hbm.1, ...), custom_call_target="tpu_custom_call" | custom-call | tf_op jit(solution)/shard_map/pallas_call | solution.py:561
  87.3 0.0 copy-start.1
  87.3 1.9 %copy.15 = bf16[1,224,1024]{2,1,0:T(8,128)(2,1)} copy(bf16[1,224,1024]{2,1,0:T(8,128)(2,1)} %get-tuple-element.16) | data formatting | bytes 917504
  89.2 0.0 copy-done.1
  89.2 0.0 copy-start
  89.2 0.8 copy.16
  90.0 0.4 copy-done
  90.4 0.0 copy-start.2
  90.4 0.8 copy.17
  91.1 0.0 copy-done.2
  91.1 0.6 copy.18
Async XLA Ops:
  87.3 1.9 %copy-start.1 = (bf16[1,224,1024]{2,1,0:T(8,128)(2,1)S(1)}, bf16[1,224,1024]{2,1,0:T(8,128)(2,1)}, u32[]{:S(2)}) copy-start(bf16[1,224,1024]{2,1,0:T(8,128)(2,1)} %get-tuple-element.17) | copy-start | bytes 1376260
  89.2 1.2 %copy-start = (bf16[1,224,1024]{2,1,0:T(8,128)(2,1)S(1)}, bf16[1,224,1024]{2,1,0:T(8,128)(2,1)}, u32[]{:S(2)}) copy-start(bf16[1,224,1024]{2,1,0:T(8,128)(2,1)} %get-tuple-element.18) | copy-start | bytes 1376260
  90.4 0.8 copy-start.2

commit v3 on v2

--- a/solution.py
+++ b/solution.py
@@ -12,7 +12,7 @@
 HD = 128
 TAG = 8
 SPLIT = 2
-UNROLL = 2
+UNROLL = 4
 MESH = pl.DeviceIdType.MESH
 EXACT = lax.Precision.HIGHEST
 F32 = jnp.float32
@@ -73,6 +73,8 @@
     v_part,
     own_ref,
     peer_ref,
+    step_in,
+    carry_ref,
     chain_in,
     chain_out,
     pass_ref,
@@ -87,8 +89,14 @@
     load_sem,
     pair_send,
     pair_recv,
+    step_send,
+    step_recv,
+    carry_send,
+    carry_recv,
     chain_send,
     chain_recv,
+    back_send,
+    back_recv,
     pass_send,
     pass_recv,
     sums_send,
@@ -189,29 +197,90 @@
             device_id_type=MESH,
         )
 
-    def ahead(way, index, to):
-        at = (way, lax.div(index, SPLIT), pl.ds(pl.multiple_of(lax.rem(index, SPLIT) * span, span), span))
-        return pltpu.make_async_remote_copy(
-            src_ref=chain_out.at[at],
-            dst_ref=chain_in.at[at],
+    def beside(way, chips_on):
+        return lax.rem(seq + 2 * (chips_on if way == 0 else -chips_on) + seqs, seqs)
+
+    def piece(way, index):
+        start = pl.multiple_of(lax.rem(index, SPLIT) * span, span)
+        return way, lax.div(index, SPLIT), pl.ds(start, span)
+
+    def hand_on(way, index):
+        return pltpu.make_async_remote_copy(
+            src_ref=chain_out.at[piece(way, index)],
+            dst_ref=step_in.at[piece(way, index)],
+            send_sem=step_send.at[way, index],
+            recv_sem=step_recv.at[way, index],
+            device_id={"seq": beside(way, 1)},
+            device_id_type=MESH,
+        )
+
+    def carried_on(way):
+        return pltpu.make_async_remote_copy(
+            src_ref=carry_ref.at[way, 0],
+            dst_ref=carry_ref.at[way, 1],
+            send_sem=carry_send.at[way],
+            recv_sem=carry_recv.at[way],
+            device_id={"seq": beside(way, 1)},
+            device_id_type=MESH,
+        )
+
+    def ahead(way, index):
+        return pltpu.make_async_remote_copy(
+            src_ref=chain_out.at[piece(way, index)],
+            dst_ref=chain_in.at[piece(way, index)],
             send_sem=chain_send.at[way, index],
             recv_sem=chain_recv.at[way, index],
-            device_id={"seq": to},
+            device_id={"seq": beside(way, 2)},
+            device_id_type=MESH,
+        )
+
+    def back(way, index):
+        return pltpu.make_async_remote_copy(
+            src_ref=chain_in.at[piece(way, index)],
+            dst_ref=chain_in.at[piece(way, index)],
+            send_sem=back_send.at[way, index],
+            recv_sem=back_recv.at[way, index],
+            device_id={"seq": beside(way, -1)},
             device_id_type=MESH,
         )
 
     def across(way, index):
-        at = (way, lax.div(index, SPLIT), pl.ds(pl.multiple_of(lax.rem(index, SPLIT) * span, span), span))
-        return pltpu.make_async_remote_copy(
-            src_ref=pass_ref.at[at],
-            dst_ref=far_ref.at[at],
+        return pltpu.make_async_remote_copy(
+            src_ref=pass_ref.at[piece(way, index)],
+            dst_ref=far_ref.at[piece(way, index)],
             send_sem=pass_send.at[way, index],
             recv_sem=pass_recv.at[way, index],
             device_id={"seq": peer},
             device_id_type=MESH,
         )
 
-    def join(way, first, has_next):
+    def each_chunk(body):
+        def turn(index, carried):
+            body(index)
+            return carried
+
+        lax.fori_loop(0, chunks, turn, 0)
+
+    ways = []
+    for way in (0, 1):
+        order = chip if way == 0 else chips - 1 - chip
+        second = lax.rem(order, 2) == 1
+        inner = order >= 2
+        ways.append(
+            (
+                core == way,
+                second,
+                jnp.logical_not(second),
+                inner,
+                jnp.logical_and(second, inner),
+                jnp.logical_and(jnp.logical_not(second), inner),
+                jnp.logical_and(second, order < chips - 1),
+                jnp.logical_and(second, order == 1),
+            )
+        )
+
+    def join(way):
+        lead, second, opening = ways[way][:3]
         exchange(way).wait_recv()
 
         def joined(local, carried):
@@ -219,57 +288,84 @@
             theirs = peer_ref[way, local, 0:HD, :]
             my_carry = own_ref[way, core * half + local, HD : HD + 1, :]
             their_carry = peer_ref[way, local, HD : HD + 1, :]
+            carry_ref[way, 0, pl.ds(local, 1), :] = my_carry * their_carry
             chain_out[way, local] = jnp.where(
-                first, their_carry * mine + theirs, my_carry * theirs + mine
+                lead, their_carry * mine + theirs, my_carry * theirs + mine
             )
             return carried
 
-        @pl.when(has_next)
+        lax.fori_loop(0, half, joined, 0)
+
+        @pl.when(opening)
         def _():
-            lax.fori_loop(0, half, joined, 0)
-
-    def chain(way, first, has_prev, has_next, to):
-        @pl.when(jnp.logical_not(has_prev))
+            each_chunk(lambda index: hand_on(way, index).start())
+            carried_on(way).start()
+            step_in[way] = jnp.zeros(step_in.shape[1:], F32)
+            carry_ref[way, 1] = jnp.ones(carry_ref.shape[2:], F32)
+
+    def pair_up(way):
+        second, onward, inner = ways[way][1], ways[way][6], ways[way][3]
+
+        @pl.when(second)
+        def _():
+            carried_on(way).wait_recv()
+
+            def body(index):
+                at = piece(way, index)
+                hand_on(way, index).wait_recv()
+                chain_out[at] = carry_ref[way, 0, pl.ds(at[1], 1), :] * step_in[at] + chain_out[at]
+
+                @pl.when(jnp.logical_and(onward, jnp.logical_not(inner)))
+                def _():
+                    ahead(way, index).start()
+
+            each_chunk(body)
+
+        @pl.when(jnp.logical_not(inner))
         def _():
             chain_in[way] = jnp.zeros(chain_in.shape[1:], F32)
 
-        def turn(index, carried):
-            local = lax.div(index, SPLIT)
-            rows = pl.ds(pl.multiple_of(lax.rem(index, SPLIT) * span, span), span)
+    def chain(way):
+        lead, second, opening, inner, second_inner, opening_inner, onward, seed = ways[way]
+
+        def body(index):
+            at = piece(way, index)
+            local, rows = at[1:]
+
+            @pl.when(second_inner)
+            def _():
+                ahead(way, index).wait_recv()
+
+                @pl.when(onward)
+                def _():
+                    both = carry_ref[way, 0, pl.ds(local, 1), :] * carry_ref[way, 1, pl.ds(local, 1), :]
+                    chain_out[at] = both * chain_in[at] + chain_out[at]
+                    ahead(way, index).start()
+
+                back(way, index).start()
+
+            @pl.when(opening_inner)
+            def _():
+                back(way, index).wait_recv()
+
             my_carry = own_ref[way, core * half + local, HD : HD + 1, :]
             their_carry = peer_ref[way, local, HD : HD + 1, :]
-
-            @pl.when(has_prev)
-            def _():
-                ahead(way, index, to).wait_recv()
-
-            state = chain_in[way, local, rows, :]
-
-            @pl.when(has_next)
-            def _():
-                chain_out[way, local, rows, :] = (
-                    my_carry * their_carry * state + chain_out[way, local, rows, :]
-                )
-                ahead(way, index, to).start()
-
+            state = carry_ref[way, 1, pl.ds(local, 1), :] * chain_in[at] + step_in[at]
             mine = own_ref[way, core * half + local, rows, :]
             theirs = peer_ref[way, local, rows, :]
-            middle = jnp.where(first, my_carry * state + mine, their_carry * state + theirs)
-            pass_ref[way, local, rows, :] = jnp.where(first, middle, state)
+            middle = jnp.where(lead, my_carry * state + mine, their_carry * state + theirs)
+            pass_ref[at] = jnp.where(lead, middle, state)
             across(way, index).start()
-            state_ref[way, core * half + local, rows, :] = jnp.where(first, state, middle).astype(BF16)
-            return carried
-
-        lax.fori_loop(0, chunks, turn, 0)
-
-        def land(index, carried):
-            local = lax.div(index, SPLIT)
-            rows = pl.ds(pl.multiple_of(lax.rem(index, SPLIT) * span, span), span)
+            state_ref[way, core * half + local, rows, :] = jnp.where(lead, state, middle).astype(BF16)
+
+        each_chunk(body)
+
+        def land(index):
+            at = piece(way, index)
             across(way, index).wait_recv()
-            state_ref[way, other * half + local, rows, :] = far_ref[way, local, rows, :].astype(BF16)
-            return carried
-
-        lax.fori_loop(0, chunks, land, 0)
+            state_ref[way, other * half + at[1], at[2], :] = far_ref[at].astype(BF16)
+
+        each_chunk(land)
 
     loads[1].wait()
     loads[2].wait()
@@ -303,16 +399,16 @@
             entered_ref[head] = entered
             attn_ref[head] = value
 
-    early = chips // 2 - 1
-
-    @pl.when(chip >= early)
+    join(0)
+
+    @pl.when(ways[0][3])
     def _():
         each_head(near, 0, heads)
 
-    join(0, core == 0, chip < chips - 1)
-    chain(0, core == 0, chip > 0, chip < chips - 1, lax.rem(seq + 2, seqs))
-
-    @pl.when(chip < early)
+    pair_up(0)
+    chain(0)
+
+    @pl.when(jnp.logical_not(ways[0][3]))
     def _():
         each_head(near, 0, heads)
 
@@ -486,27 +582,32 @@
         gain_far[0] = total / math.sqrt(blk * seqs * rows_of)
         gain_pass.start()
 
-    late = chips - early
-    back = (core == 1, chip < chips - 1, chip > 0, lax.rem(seq + seqs - 2, seqs))
-
-    @pl.when(chip < late)
+    far_on = chips - 1 - chip >= 4
+
+    @pl.when(ways[1][3])
     def _():
         each_head(masked, 0, half)
-        join(1, core == 1, chip > 0)
-        gain_begin()
+
+    join(1)
+    gain_begin()
+
+    @pl.when(ways[1][3])
+    def _():
         each_head(masked, half, half)
+
+    @pl.when(far_on)
+    def _():
         gain_middle()
 
-    @pl.when(chip >= late)
-    def _():
-        join(1, core == 1, chip > 0)
-        gain_begin()
-
-    chain(1, *back)
-
-    @pl.when(chip >= late)
+    pair_up(1)
+    chain(1)
+
+    @pl.when(jnp.logical_not(ways[1][3]))
     def _():
         each_head(masked, 0, heads)
+
+    @pl.when(jnp.logical_not(far_on))
+    def _():
         gain_middle()
 
     gain_end()
@@ -534,18 +635,30 @@
     each_step(rows_of, lambda step: over_rows(step).wait_send())
     for share in shares:
         share.wait_send()
-    for way, has_next in ((0, chip < chips - 1), (1, chip > 0)):
+    for way in (0, 1):
         exchange(way).wait_send()
-
-        def sent(index, carried, way=way, has_next=has_next):
-            @pl.when(has_next)
-            def _():
-                ahead(way, index, peer).wait_send()
-
-            across(way, index).wait_send()
-            return carried
-
-        lax.fori_loop(0, chunks, sent, 0)
+        opening, second_inner, onward = ways[way][2], ways[way][4], ways[way][6]
+
+        @pl.when(opening)
+        def _(way=way):
+            carried_on(way).wait_send()
+            each_chunk(lambda index: hand_on(way, index).wait_send())
+
+        @pl.when(onward)
+        def _(way=way):
+            each_chunk(lambda index: ahead(way, index).wait_send())
+
+        @pl.when(second_inner)
+        def _(way=way):
+            each_chunk(lambda index: back(way, index).wait_send())
+
+        each_chunk(lambda index, way=way: across(way, index).wait_send())
+
+
+def deliver(*refs):
+    count = len(refs) // 2
+    for one in range(count):
+        refs[count + one][...] = refs[one][...]
 
 
 def on_device(seqs, teams, rows_of, queries, keys_in, values_in, grad_output, log_decay, lengths, norm_gain):
@@ -586,12 +699,14 @@
             pltpu.VMEM((2, heads, HD + TAG, HD), F32),
             pltpu.VMEM((2, half, HD + TAG, HD), F32),
             states,
+            pltpu.VMEM((2, 2, half, HD), F32),
+            states,
             states,
             states,
             states,
             pltpu.VMEM((2, heads, HD, HD), BF16),
             pltpu.VMEM((16, tokens), F32),
-            pltpu.VMEM((teams - 1, 16, tokens), F32),
+            pltpu.VMEM((max(teams - 1, 1), 16, tokens), F32),
             pltpu.VMEM((heads, HD), F32),
             pltpu.VMEM((seqs // 2, half, HD), F32),
             pltpu.VMEM((rows_of, half, HD), F32),
@@ -601,13 +716,19 @@
             pltpu.SemaphoreType.DMA((2,)),
             pltpu.SemaphoreType.DMA((2, chunks)),
             pltpu.SemaphoreType.DMA((2, chunks)),
+            pltpu.SemaphoreType.DMA((2,)),
+            pltpu.SemaphoreType.DMA((2,)),
             pltpu.SemaphoreType.DMA((2, chunks)),
             pltpu.SemaphoreType.DMA((2, chunks)),
-            pltpu.SemaphoreType.DMA((teams - 1,)),
-            pltpu.SemaphoreType.DMA((teams - 1,)),
-            pltpu.SemaphoreType.DMA((seqs // 2 - 1,)),
+            pltpu.SemaphoreType.DMA((2, chunks)),
+            pltpu.SemaphoreType.DMA((2, chunks)),
+            pltpu.SemaphoreType.DMA((2, chunks)),
+            pltpu.SemaphoreType.DMA((2, chunks)),
+            pltpu.SemaphoreType.DMA((max(teams - 1, 1),)),
+            pltpu.SemaphoreType.DMA((max(teams - 1, 1),)),
+            pltpu.SemaphoreType.DMA((max(seqs // 2 - 1, 1),)),
             pltpu.SemaphoreType.DMA((seqs // 2,)),
-            pltpu.SemaphoreType.DMA((rows_of - 1,)),
+            pltpu.SemaphoreType.DMA((max(rows_of - 1, 1),)),
             pltpu.SemaphoreType.DMA((rows_of,)),
             pltpu.SemaphoreType.DMA((2,)),
         ],
@@ -623,6 +744,14 @@
         lengths,
         norm_gain.reshape(heads, HD),
     )
+    made = (query_grad, key_grad, value_grad, gain)
+    any_space = pl.BlockSpec(memory_space=pltpu.VMEM)
+    query_grad, key_grad, value_grad, gain = pl.pallas_call(
+        deliver,
+        out_shape=tuple(jax.ShapeDtypeStruct(one.shape, one.dtype) for one in made),
+        in_specs=[any_space] * 4,
+        out_specs=[any_space] * 4,
+    )(*made)
     return query_grad, key_grad, value_grad, gain.reshape(features)
 
 

time: 92 us -> 85.4 us (0.928)
  the two profiles are of different devices: /device:TPU:1 before, /device:TPU:9 now
where the time goes in v3:
time: 85.4 us; the launch traced here: 85.2 us
  Pallas kernels  84.6 us (99%)
    pallas_call x1, Pallas kernels, on_device(): pl.pallas_call(functools.partial(kernel, seqs, teams, rows_of), out_shape...  82.2 us
    pallas_call x1, Pallas kernels, on_device(): pl.pallas_call(deliver, out_shape=tuple((jax.ShapeDtypeStruct(one.shape,...  2.4 us

profile of v3, /device:TPU:9, one launch (start us, length us, event | category | flops | bytes accessed | tf_op | source)
XLA Modules:
  0.0 85.2 jit_solution(16696603710067135389)
XLA Ops:
  0.6 82.2 %shard_map.102 = (bf16[1,224,1024]{2,1,0:T(8,128)(2,1)}, bf16[1,224,1024]{2,1,0:T(8,128)(2,1)}, bf16[1,224,1024]{2,1,0:T(8,128)(2,1)}, f32[8,128]{1,0:T(8,128)}) custom-call(bf16[1,224,1024]{2,1,0:T(8,128)(2,1)} %q_hbm.1, bf16[1,224,1024]{2,1,0:T(8,128)(2,1)} %k_hbm.1, bf16[1,224,1024]{2,1,0:T(8,128)(2,1)} %v_hbm.1, bf16[1,224,1024]{2,1,0:T(8,128)(2,1)} %up_hbm.1, ...), custom_call_target="tpu_custom_call" | custom-call | tf_op jit(solution)/shard_map/pallas_call | solution.py:674
  82.8 2.4 %shard_map.103 = (bf16[1,224,1024]{2,1,0:T(8,128)(2,1)}, bf16[1,224,1024]{2,1,0:T(8,128)(2,1)}, bf16[1,224,1024]{2,1,0:T(8,128)(2,1)}, f32[8,128]{1,0:T(8,128)}) custom-call(bf16[1,224,1024]{2,1,0:T(8,128)(2,1)} %get-tuple-element.12.refs_0_, bf16[1,224,1024]{2,1,0:T(8,128)(2,1)} %get-tuple-element.13.refs_1_, ...), custom_call_target="tpu_custom_call" | custom-call | tf_op jit(solution)/shard_map/pallas_call | solution.py:749

commit v4 on v3

--- a/solution.py
+++ b/solution.py
@@ -13,6 +13,7 @@
 TAG = 8
 SPLIT = 2
 UNROLL = 4
+REACH = 4
 MESH = pl.DeviceIdType.MESH
 EXACT = lax.Precision.HIGHEST
 F32 = jnp.float32
@@ -106,6 +107,7 @@
     gain_rows_send,
     gain_rows_recv,
     gain_far_sem,
+    told_sem,
 ):
     blk, features = q_ref.shape
     heads = features // HD
@@ -142,13 +144,42 @@
             barrier, inc=1, device_id={"seq": lax.rem(seq + 2 * step, seqs)}, device_id_type=MESH
         )
 
-    def greet(step, carried):
-        pl.semaphore_signal(
-            barrier, inc=1, device_id={"dp": lax.rem(place_z + step, rows_of)}, device_id_type=MESH
-        )
-        return carried
-
-    lax.fori_loop(1, rows_of, greet, 0)
+    def each_along_z(distance, action):
+        for side, place in enumerate((place_z - distance, place_z + distance)):
+
+            @pl.when(jnp.logical_and(place >= 0, place < rows_of))
+            def _(side=side, place=place):
+                action(side, place)
+
+    close = min(REACH, rows_of - 1)
+    for distance in range(1, close + 1):
+        each_along_z(
+            distance,
+            lambda side, place: pl.semaphore_signal(
+                barrier, inc=1, device_id={"dp": place}, device_id_type=MESH
+            ),
+        )
+    greeted = 1 + teams - 1 + chips - 1
+    for distance in range(1, close + 1):
+        greeted = greeted + jnp.where(place_z >= distance, 1, 0)
+        greeted = greeted + jnp.where(place_z + distance < rows_of, 1, 0)
+
+    def tell(turn):
+        each_along_z(
+            REACH << turn,
+            lambda side, place: pl.semaphore_signal(
+                told_sem.at[turn, side], inc=1, device_id={"dp": place}, device_id_type=MESH
+            ),
+        )
+
+    def hear(turn):
+        each_along_z(
+            REACH << turn, lambda side, place: pl.semaphore_wait(told_sem.at[turn, 1 - side], 1)
+        )
+
+    turns = 0
+    while REACH << turns < rows_of:
+        turns += 1
 
     def lanes(head):
         return pl.ds(pl.multiple_of(head * HD, HD), HD)
@@ -370,8 +401,10 @@
     loads[1].wait()
     loads[2].wait()
     each_head(block_state, other * half, half)
-    pl.semaphore_wait(barrier, 1 + teams - 1 + chips - 1 + rows_of - 1)
+    pl.semaphore_wait(barrier, greeted)
     exchange(0).start()
+    if turns:
+        tell(0)
     each_head(block_state, core * half, half)
 
     c_row[...] = dot(log, triangle, 1, 1, EXACT)
@@ -411,6 +444,10 @@
     @pl.when(jnp.logical_not(ways[0][3]))
     def _():
         each_head(near, 0, heads)
+
+    for turn in range(1, turns):
+        hear(turn - 1)
+        tell(turn)
 
     squares_ref[...] = jnp.zeros_like(squares_ref)
     inner_ref[...] = jnp.zeros_like(inner_ref)
@@ -558,6 +595,8 @@
         each_step(chips, lambda step: over_chips(step).start())
 
     def gain_middle():
+        if turns:
+            hear(turns - 1)
         each_step(chips, lambda step: from_chips(step).wait_recv())
         total = gain_chips[0]
         for one in range(1, chips):
@@ -731,6 +770,7 @@
             pltpu.SemaphoreType.DMA((max(rows_of - 1, 1),)),
             pltpu.SemaphoreType.DMA((rows_of,)),
             pltpu.SemaphoreType.DMA((2,)),
+            pltpu.SemaphoreType.REGULAR((8, 2)),
         ],
         compiler_params=pltpu.CompilerParams(
             collective_id=0, has_side_effects=True, vmem_limit_bytes=63 * 1024 * 1024

time: 85.4 us -> 83.9 us (0.982)
  the two profiles are of different devices: /device:TPU:9 before, /device:TPU:41 now
where the time goes in v4:
time: 83.9 us; the launch traced here: 83.7 us
  Pallas kernels  83 us (99%)
    pallas_call x1, Pallas kernels, on_device(): pl.pallas_call(functools.partial(kernel, seqs, teams, rows_of), out_shape...  80.6 us
    pallas_call x1, Pallas kernels, on_device(): pl.pallas_call(deliver, out_shape=tuple((jax.ShapeDtypeStruct(one.shape,...  2.4 us

profile of v4, /device:TPU:41, one launch (start us, length us, event | category | flops | bytes accessed | tf_op | source)
XLA Modules:
  0.0 83.7 jit_solution(18382592345652063588)
XLA Ops:
  0.6 80.6 %shard_map.102 = (bf16[1,224,1024]{2,1,0:T(8,128)(2,1)}, bf16[1,224,1024]{2,1,0:T(8,128)(2,1)}, bf16[1,224,1024]{2,1,0:T(8,128)(2,1)}, f32[8,128]{1,0:T(8,128)}) custom-call(bf16[1,224,1024]{2,1,0:T(8,128)(2,1)} %q_hbm.1, bf16[1,224,1024]{2,1,0:T(8,128)(2,1)} %k_hbm.1, bf16[1,224,1024]{2,1,0:T(8,128)(2,1)} %v_hbm.1, bf16[1,224,1024]{2,1,0:T(8,128)(2,1)} %up_hbm.1, ...), custom_call_target="tpu_custom_call" | custom-call | tf_op jit(solution)/shard_map/pallas_call | solution.py:713
  81.3 2.4 %shard_map.103 = (bf16[1,224,1024]{2,1,0:T(8,128)(2,1)}, bf16[1,224,1024]{2,1,0:T(8,128)(2,1)}, bf16[1,224,1024]{2,1,0:T(8,128)(2,1)}, f32[8,128]{1,0:T(8,128)}) custom-call(bf16[1,224,1024]{2,1,0:T(8,128)(2,1)} %get-tuple-element.12.refs_0_, bf16[1,224,1024]{2,1,0:T(8,128)(2,1)} %get-tuple-element.13.refs_1_, ...), custom_call_target="tpu_custom_call" | custom-call | tf_op jit(solution)/shard_map/pallas_call | solution.py:789

commit v5 on v4

--- a/solution.py
+++ b/solution.py
@@ -621,35 +621,37 @@
         gain_far[0] = total / math.sqrt(blk * seqs * rows_of)
         gain_pass.start()
 
-    far_on = chips - 1 - chip >= 4
-
-    @pl.when(ways[1][3])
+    far_on = ways[1][3]
+
+    @pl.when(far_on)
     def _():
         each_head(masked, 0, half)
 
     join(1)
     gain_begin()
 
-    @pl.when(ways[1][3])
+    @pl.when(far_on)
     def _():
         each_head(masked, half, half)
+
+    pair_up(1)
 
     @pl.when(far_on)
     def _():
         gain_middle()
 
-    pair_up(1)
     chain(1)
-
-    @pl.when(jnp.logical_not(ways[1][3]))
-    def _():
-        each_head(masked, 0, heads)
 
     @pl.when(jnp.logical_not(far_on))
     def _():
         gain_middle()
-
-    gain_end()
+        each_head(masked, 0, heads)
+
+    last = chips - 1 - chip >= 4
+
+    @pl.when(last)
+    def _():
+        gain_end()
 
     def finish(group):
         made = []
@@ -664,6 +666,11 @@
             v_out[0, :, lanes(head)] = value
 
     each_head(finish, 0, heads)
+
+    @pl.when(jnp.logical_not(last))
+    def _():
+        gain_end()
+
 
     gain_pass.wait_recv()
     for local in range(half):

time: 83.9 us -> 81.1 us (0.967)
  the two profiles are of different devices: /device:TPU:41 before, /device:TPU:9 now
where the time goes in v5:
time: 81.1 us; the launch traced here: 80.9 us
  Pallas kernels  80.2 us (99%)
    pallas_call x1, Pallas kernels, on_device(): pl.pallas_call(functools.partial(kernel, seqs, teams, rows_of), out_shape...  77.8 us
    pallas_call x1, Pallas kernels, on_device(): pl.pallas_call(deliver, out_shape=tuple((jax.ShapeDtypeStruct(one.shape,...  2.4 us

profile of v5, /device:TPU:9, one launch (start us, length us, event | category | flops | bytes accessed | tf_op | source)
XLA Modules:
  0.0 80.9 jit_solution(6864828399906194966)
XLA Ops:
  0.6 77.8 %shard_map.102 = (bf16[1,224,1024]{2,1,0:T(8,128)(2,1)}, bf16[1,224,1024]{2,1,0:T(8,128)(2,1)}, bf16[1,224,1024]{2,1,0:T(8,128)(2,1)}, f32[8,128]{1,0:T(8,128)}) custom-call(bf16[1,224,1024]{2,1,0:T(8,128)(2,1)} %q_hbm.1, bf16[1,224,1024]{2,1,0:T(8,128)(2,1)} %k_hbm.1, bf16[1,224,1024]{2,1,0:T(8,128)(2,1)} %v_hbm.1, bf16[1,224,1024]{2,1,0:T(8,128)(2,1)} %up_hbm.1, ...), custom_call_target="tpu_custom_call" | custom-call | tf_op jit(solution)/shard_map/pallas_call | solution.py:720
  78.5 2.4 %shard_map.103 = (bf16[1,224,1024]{2,1,0:T(8,128)(2,1)}, bf16[1,224,1024]{2,1,0:T(8,128)(2,1)}, bf16[1,224,1024]{2,1,0:T(8,128)(2,1)}, f32[8,128]{1,0:T(8,128)}) custom-call(bf16[1,224,1024]{2,1,0:T(8,128)(2,1)} %get-tuple-element.12.refs_0_, bf16[1,224,1024]{2,1,0:T(8,128)(2,1)} %get-tuple-element.13.refs_1_, ...), custom_call_target="tpu_custom_call" | custom-call | tf_op jit(solution)/shard_map/pallas_call | solution.py:796

commit v6 on v5

--- a/solution.py
+++ b/solution.py
@@ -391,6 +391,7 @@
 
         each_chunk(body)
 
+    def receive(way):
         def land(index):
             at = piece(way, index)
             across(way, index).wait_recv()
@@ -466,7 +467,9 @@
         squares_ref[...] = squares
         inner_ref[...] = inner
 
-    each_head(attend, 0, heads)
+    each_head(attend, core * half, half)
+    receive(0)
+    each_head(attend, other * half, half)
     ones = jnp.ones((8, HD), F32)
     sums_ref[0:8, :] = dot(ones, squares_ref[...], 1, 1, EXACT)
     sums_ref[8:16, :] = dot(ones, inner_ref[...], 1, 1, EXACT)
@@ -665,7 +668,9 @@
             k_out[0, :, lanes(head)] = key
             v_out[0, :, lanes(head)] = value
 
-    each_head(finish, 0, heads)
+    each_head(finish, core * half, half)
+    receive(1)
+    each_head(finish, other * half, half)
 
     @pl.when(jnp.logical_not(last))
     def _():

time: 81.1 us -> 80.6 us (level)
  no operation moved by 1% of the time
where the time goes in v6:
time: 80.6 us; the launch traced here: 80.4 us
  Pallas kernels  79.8 us (99%)
    pallas_call x1, Pallas kernels, on_device(): pl.pallas_call(functools.partial(kernel, seqs, teams, rows_of), out_shape...  77.4 us
    pallas_call x1, Pallas kernels, on_device(): pl.pallas_call(deliver, out_shape=tuple((jax.ShapeDtypeStruct(one.shape,...  2.4 us

profile of v6, /device:TPU:9, one launch (start us, length us, event | category | flops | bytes accessed | tf_op | source)
XLA Modules:
  0.0 80.4 jit_solution(10453531897447397285)
XLA Ops:
  0.6 77.4 %shard_map.102 = (bf16[1,224,1024]{2,1,0:T(8,128)(2,1)}, bf16[1,224,1024]{2,1,0:T(8,128)(2,1)}, bf16[1,224,1024]{2,1,0:T(8,128)(2,1)}, f32[8,128]{1,0:T(8,128)}) custom-call(bf16[1,224,1024]{2,1,0:T(8,128)(2,1)} %q_hbm.1, bf16[1,224,1024]{2,1,0:T(8,128)(2,1)} %k_hbm.1, bf16[1,224,1024]{2,1,0:T(8,128)(2,1)} %v_hbm.1, bf16[1,224,1024]{2,1,0:T(8,128)(2,1)} %up_hbm.1, ...), custom_call_target="tpu_custom_call" | custom-call | tf_op jit(solution)/shard_map/pallas_call | solution.py:725
  78.0 2.4 %shard_map.103 = (bf16[1,224,1024]{2,1,0:T(8,128)(2,1)}, bf16[1,224,1024]{2,1,0:T(8,128)(2,1)}, bf16[1,224,1024]{2,1,0:T(8,128)(2,1)}, f32[8,128]{1,0:T(8,128)}) custom-call(bf16[1,224,1024]{2,1,0:T(8,128)(2,1)} %get-tuple-element.12.refs_0_, bf16[1,224,1024]{2,1,0:T(8,128)(2,1)} %get-tuple-element.13.refs_1_, ...), custom_call_target="tpu_custom_call" | custom-call | tf_op jit(solution)/shard_map/pallas_call | solution.py:801
